TPU v7x, 32 devices: a whole 2x2x4 slice. The times are simulated.
32 devices in a mesh: row: 4 (over x, core), col: 8 (over z, y).
Axes of the slice: x: 2, y: 2, z: 4, core: 2. Of those that a mesh axis runs over, the one named last changes fastest.
Arguments:
- eta_pairs: bfloat16 [12288, 12288], P('row', 'col'), may hold values from -6 to 6
- gamma_pairs: bfloat16 [12288, 12288], P('row', 'col'), may hold values from -0.0546875 to 0.0546875
- pair_first: int32 [12288], P('row'), may hold values from 0 to 239
- pair_second: int32 [12288], P('row'), may hold values from 0 to 239
- occupancy: float32 [240], replicated, may hold values from 0 to 1
- gamma_recoupled: bfloat16 [32, 1536, 1536], P(('row', 'col')), may hold values from -0.15625 to 0.15625
- ph_factor: float32 [32, 1536], P(('row', 'col')), may hold values from -1 to 1
- tile_source: int32 [32, 576], P(('row', 'col')), may hold values from 0 to 287, as said below
- tile_owner: int32 [32, 576], P(('row', 'col')), may hold values from 0 to 31, as said below
- tile_place: int32 [32, 576], P(('row', 'col')), may hold values from 0 to 143
- sixj_weight: bfloat16 [32, 576], P(('row', 'col')), may hold values from -1 to 1
- live_count: int32 [32], P(('row', 'col')), may hold values from 288 to 576, as said below
Outputs:
- panel_update: bfloat16 [1024, 12288], P('col', 'row')
- recoupled_update: bfloat16 [12288, 12288], P('row', 'col')
Inputs may be any that keep to these rules, and one draw needn't show every extreme that they name: `tile_source`: in each row the first 288 entries name every tile of the block once. `tile_owner`: in each row no channel is named by more than 18 entries; one channel is named exactly 18 times within the first 288 entries of every row. `live_count`: some block has 576 live slots and another 288.
All inputs are finite; a program needn't handle non-finite values.
Results may differ from a plain program's by a relative error of at most 0.019.
Values may be sent and summed in bfloat16 or wider, within the bound.
A program may use at most 192 MiB of HBM per device.

v0:
```python
import jax
import jax.numpy as jnp
from jax import lax
from jax.sharding import PartitionSpec as P

TILE = 128
PH_STATES = 1536
PANEL_DEV = 128


def orbit_lookup(pair_ids, occupancy):
    orbit_ids = jnp.arange(occupancy.shape[0], dtype=jnp.int32)
    return jnp.sum(
        jnp.where(pair_ids[:, None] == orbit_ids[None, :], occupancy[None, :], 0.0), axis=1
    )


def panel_part(eta_pairs, gamma_pairs, pair_first, pair_second, occupancy):
    factor = 1.0 - orbit_lookup(pair_first, occupancy) - orbit_lookup(pair_second, occupancy)
    panel_width = PANEL_DEV
    gamma_cols = (
        (factor[:, None] * gamma_pairs[:, :panel_width].astype(jnp.float32)).astype(jnp.bfloat16).T
    )
    eta_cols = (
        (factor[:, None] * eta_pairs[:, :panel_width].astype(jnp.float32)).astype(jnp.bfloat16).T
    )
    gamma_whole, eta_whole = (
        lax.all_gather(gamma_cols, "row", axis=1, tiled=True),
        lax.all_gather(eta_cols, "row", axis=1, tiled=True),
    )
    gamma_panel, eta_panel = (
        lax.all_to_all(gamma_whole, "col", split_axis=1, concat_axis=0, tiled=True),
        lax.all_to_all(eta_whole, "col", split_axis=1, concat_axis=0, tiled=True),
    )
    contract = (((1,), (1,)), ((), ()))
    leading = lax.dot_general(gamma_panel, eta_pairs, contract, preferred_element_type=jnp.float32)
    trailing = lax.dot_general(eta_panel, gamma_pairs, contract, preferred_element_type=jnp.float32)
    return lax.psum_scatter(
        (leading - trailing).astype(jnp.bfloat16), "col", scatter_dimension=0, tiled=True
    )


def deliver(sent_tiles, place_code):
    moved_tiles, moved_codes = (
        lax.all_to_all(sent_tiles, ("row", "col"), split_axis=0, concat_axis=0, tiled=True),
        lax.all_to_all(place_code, ("row", "col"), split_axis=0, concat_axis=0, tiled=True),
    )
    return (moved_tiles, moved_codes)


def collect(answer_tiles):
    return lax.all_to_all(answer_tiles, ("row", "col"), split_axis=0, concat_axis=0, tiled=True)


def recoupled_part(
    eta_pairs,
    gamma_recoupled,
    ph_factor,
    tile_source,
    tile_owner,
    tile_place,
    sixj_weight,
    live_count,
):
    n_row = lax.axis_size("row")
    n_col = lax.axis_size("col")
    blocks = n_row * n_col
    slot_total = tile_source.shape[1]
    capacity = max(2, (slot_total + blocks - 1) // blocks)
    row_tiles = eta_pairs.shape[0] // TILE
    col_tiles = eta_pairs.shape[1] // TILE
    block_tiles = row_tiles * col_tiles
    ph_tiles = PH_STATES // TILE
    tile_area = TILE * TILE
    eta_tiles = (
        eta_pairs.reshape(row_tiles, TILE, col_tiles, TILE)
        .transpose(0, 2, 1, 3)
        .reshape(block_tiles, tile_area)
    )
    sources = tile_source[0]
    owners = tile_owner[0]
    places = tile_place[0]
    weights = sixj_weight[0].astype(jnp.float32)
    slot_ids = jnp.arange(slot_total, dtype=jnp.int32)
    is_live = slot_ids < live_count[0]
    same_owner = (
        (owners[:, None] == owners[None, :])
        & is_live[None, :]
        & (slot_ids[None, :] < slot_ids[:, None])
    )
    slot_rank = jnp.sum(same_owner.astype(jnp.int32), axis=1)
    buffer_ids = jnp.arange(blocks * capacity, dtype=jnp.int32)
    slot_hit = (
        ((owners * capacity + slot_rank)[:, None] == buffer_ids[None, :]) & is_live[:, None]
    ).astype(jnp.float32)
    tile_ids = jnp.arange(block_tiles, dtype=jnp.int32)
    source_hit = (sources[:, None] == tile_ids[None, :]).astype(jnp.float32) * weights[:, None]
    highest = lax.Precision.HIGHEST
    lead_dims = (((0,), (0,)), ((), ()))
    outward = lax.dot_general(slot_hit, source_hit, lead_dims, precision=highest).astype(
        jnp.bfloat16
    )
    sent_tiles = jnp.dot(outward, eta_tiles, preferred_element_type=jnp.float32).astype(
        jnp.bfloat16
    )
    place_code = (
        lax.dot_general(slot_hit, places.astype(jnp.float32) + 1.0, lead_dims, precision=highest)
        - 1.0
    )
    place_code = place_code.astype(jnp.bfloat16)
    received, codes = deliver(
        sent_tiles.reshape(blocks, capacity, tile_area), place_code.reshape(blocks, capacity)
    )
    received = received.reshape(blocks * capacity, tile_area)
    codes = codes.reshape(blocks * capacity).astype(jnp.float32)
    positions = jnp.arange(ph_tiles * ph_tiles, dtype=jnp.float32)
    assemble = (positions[:, None] == codes[None, :]).astype(jnp.bfloat16)
    eta_ph = jnp.dot(assemble, received, preferred_element_type=jnp.float32).astype(jnp.bfloat16)
    eta_ph = (
        eta_ph.reshape(ph_tiles, ph_tiles, TILE, TILE)
        .transpose(0, 2, 1, 3)
        .reshape(PH_STATES, PH_STATES)
    )
    gamma_ph = gamma_recoupled[0]
    scale = ph_factor[0]
    gamma_scaled = (scale[:, None] * gamma_ph.astype(jnp.float32)).astype(jnp.bfloat16)
    eta_scaled = (scale[:, None] * eta_ph.astype(jnp.float32)).astype(jnp.bfloat16)
    product = jnp.dot(eta_ph, gamma_scaled, preferred_element_type=jnp.float32)
    product = (product - jnp.dot(gamma_ph, eta_scaled, preferred_element_type=jnp.float32)).astype(
        jnp.bfloat16
    )
    product_tiles = (
        product.reshape(ph_tiles, TILE, ph_tiles, TILE)
        .transpose(0, 2, 1, 3)
        .reshape(ph_tiles * ph_tiles, tile_area)
    )
    answer = lax.dot_general(
        assemble, product_tiles, lead_dims, preferred_element_type=jnp.float32
    ).astype(jnp.bfloat16)
    returned = collect(answer.reshape(blocks, capacity, tile_area)).reshape(
        blocks * capacity, tile_area
    )
    inward = lax.dot_general(source_hit, slot_hit, lead_dims, precision=highest).astype(
        jnp.bfloat16
    )
    update = jnp.dot(inward, returned, preferred_element_type=jnp.float32).astype(jnp.bfloat16)
    return (
        update.reshape(row_tiles, col_tiles, TILE, TILE)
        .transpose(0, 2, 1, 3)
        .reshape(eta_pairs.shape)
    )


def local(
    eta_pairs,
    gamma_pairs,
    pair_first,
    pair_second,
    occupancy,
    gamma_recoupled,
    ph_factor,
    tile_source,
    tile_owner,
    tile_place,
    sixj_weight,
    live_count,
):
    panel_update = panel_part(eta_pairs, gamma_pairs, pair_first, pair_second, occupancy)
    recoupled_update = recoupled_part(
        eta_pairs,
        gamma_recoupled,
        ph_factor,
        tile_source,
        tile_owner,
        tile_place,
        sixj_weight,
        live_count,
    )
    return (panel_update, recoupled_update)


def solution(mesh):
    in_specs = (
        P("row", "col"),
        P("row", "col"),
        P("row"),
        P("row"),
        P(),
        P(("row", "col"), None, None),
        P(("row", "col"), None),
        P(("row", "col"), None),
        P(("row", "col"), None),
        P(("row", "col"), None),
        P(("row", "col"), None),
        P(("row", "col")),
    )
    out_specs = (P("col", "row"), P("row", "col"))
    return jax.shard_map(local, mesh=mesh, in_specs=in_specs, out_specs=out_specs, check_vma=False)
```

profile of v0, /device:TPU:0, one launch (start us, length us, event | category | flops | bytes accessed | tf_op | source)
XLA Modules:
  0.0 1546.2 jit_solution(15761078547057051556)
XLA Ops:
  7.8 0.7 reduce.2
  8.9 1.4 fusion.32
  10.3 0.7 all_to_all.52
  11.0 7.3 all-to-all-start.2
  18.3 0.7 convert_reduce_fusion.2
  19.0 0.7 reduce
  19.7 12.6 copy.45
  32.3 9.8 copy.53
  42.1 13.1 copy.46
  55.2 1.6 fusion.27
  56.9 19.1 %convolution_convert_fusion = bf16[576,16384]{1,0:T(8,128)(2,1)} fusion(bf16[576,288]{0,1:T(8,128)(2,1)S(1)} %fusion.27, bf16[36,8,128,128]{3,2,1,0:T(8,128)(2,1)} %bitcast.84), kind=kOutput, calls=%fused_computation | convolution fusion | flops 5445255168 | bytes 28643328 | tf_op jit(solution)/shard_map/dot_general | solution.py:103
  75.9 18.4 %reshape.112 = bf16[32,18,16384]{2,1,0:T(8,128)(2,1)} reshape(bf16[576,16384]{1,0:T(8,128)(2,1)} %convolution_convert_fusion) | data formatting | bytes 37748736 | tf_op jit(solution)/shard_map/reshape | solution.py:112
  94.3 6.0 all-to-all-start.3
  100.4 0.9 select_reduce_fusion.1
  101.3 3.0 fusion.36
  104.3 108.2 %all-gather.3.cloned.1.call-done = bf16[128,12288]{0,1:T(8,128)(2,1)} async-done(((bf16[128,3072]{0,1:T(8,128)(2,1)}), bf16[128,12288]{0,1:T(8,128)(2,1)}) %all-gather.3.cloned.1.call-update) | async-done | bytes 3145744 | tf_op jit(solution)/shard_map/all_gather | solution.py:28
  212.6 446.7 %all-to-all-done.3 = bf16[32,18,16384]{2,1,0:T(8,128)(2,1)} async-done(((bf16[32,18,16384]{2,1,0:T(8,128)(2,1)}), bf16[32,18,16384]{2,1,0:T(8,128)(2,1)}, u32[]{:S(2)}, u32[]{:S(2)}) %all-to-all-start.3) | async-done | bytes 18874400 | tf_op jit(solution)/shard_map/all_to_all | solution.py:45
  659.2 3.6 all-to-all-start
  662.9 0.7 all-gather.5.cloned.1.call-update
  663.8 18.6 %reshape.113 = bf16[576,16384]{1,0:T(8,128)(2,1)} reshape(bf16[32,18,16384]{2,1,0:T(8,128)(2,1)} %all-to-all-done.3) | data formatting | bytes 37748736 | tf_op jit(solution)/shard_map/reshape | solution.py:114
  682.5 10.3 fusion.15
  692.8 1.4 copy.55
  694.2 2.2 copy-done
  696.4 7.1 multiply_convert_fusion
  703.5 30.3 %all-to-all-done = bf16[128,8,1536]{0,2,1:T(8,128)(2,1)S(1)} async-done(((bf16[128,8,1536]{0,2,1:T(8,128)(2,1)}), bf16[128,8,1536]{0,2,1:T(8,128)(2,1)S(1)}, u32[]{:S(2)}, u32[]{:S(2)}) %all-to-all-start) | async-done | bytes 3145760 | tf_op jit(solution)/shard_map/all_to_all | solution.py:32
  733.8 1.6 copy-done.1
  735.4 5.0 all-to-all-start.1
  740.4 13.5 fusion.8
  754.0 3.7 copy.47
  757.6 12.8 fusion.2
  770.4 9.4 reshape.116
  779.8 4.1 copy.49
  784.0 15.0 convolution_convert_fusion.1
  799.0 18.2 %reshape.118 = bf16[32,18,16384]{2,1,0:T(8,128)(2,1)} reshape(bf16[576,16384]{1,0:T(8,128)(2,1)} %convolution_convert_fusion.1) | data formatting | bytes 37748736 | tf_op jit(solution)/shard_map/reshape | solution.py:140
  817.3 5.6 all-to-all-start.4
  822.9 3.0 copy.42
  825.9 4.8 copy.43
  830.7 15.1 fusion.58
  845.8 17.8 %subtract_convert_fusion = bf16[1024,3072]{1,0:T(8,128)(2,1)} fusion(f32[1024,3072]{1,0:T(8,128)} %fusion.58, bf16[1024,1536]{1,0:T(8,128)(2,1)} %bitcast.98, bf16[3072,1536]{1,0:T(8,128)(2,1)} %param.13), kind=kOutput, calls=%fused_computation.5 | convolution fusion | flops 9669967872 | bytes 31457280 | tf_op jit(solution)/shard_map/dot_general | solution.py:37
  863.6 0.6 copy-done.8
  864.3 1.6 fusion.24
  865.9 592.4 %all-to-all-done.4 = bf16[32,18,16384]{2,1,0:T(8,128)(2,1)} async-done(((bf16[32,18,16384]{2,1,0:T(8,128)(2,1)}), bf16[32,18,16384]{2,1,0:T(8,128)(2,1)}, u32[]{:S(2)}, u32[]{:S(2)}) %all-to-all-start.4) | async-done | bytes 18874400 | tf_op jit(solution)/shard_map/all_to_all | solution.py:52
  1458.2 18.4 %reshape.119 = bf16[576,16384]{1,0:T(8,128)(2,1)} reshape(bf16[32,18,16384]{2,1,0:T(8,128)(2,1)} %all-to-all-done.4) | data formatting | bytes 37748736 | tf_op jit(solution)/shard_map/reshape | solution.py:140
  1476.6 16.9 %fusion.3 = bf16[36,8,128,128]{3,1,2,0:T(8,128)(2,1)} fusion(bf16[288,576]{1,0:T(8,128)(2,1)S(1)} %fusion.24, bf16[576,16384]{1,0:T(8,128)(2,1)} %reshape.119), kind=kOutput, calls=%fused_computation.12 | convolution fusion | flops 5440536576 | bytes 28643328 | tf_op jit(solution)/shard_map/dot_general | solution.py:146
  1493.5 10.2 copy.59
  1503.7 13.1 copy.50
  1516.8 9.8 copy.79
  1526.6 12.6 copy.51
  (51 shorter events, 0.8 us)
Async XLA Ops:
  7.8 47.4 %copy-start.14 = (pred[576]{0:T(1024)(128)(4,1)}, pred[576]{0:T(1024)(128)(4,1)S(1)}, u32[]{:S(2)}) copy-start(pred[576]{0:T(1024)(128)(4,1)S(1)} %iota_compare_fusion.10) | copy-start | bytes 1732
  8.9 46.4 %copy-start.7 = (s32[576]{0:T(1024)}, s32[576]{0:T(1024)S(1)}, u32[]{:S(2)}) copy-start(s32[576]{0:T(1024)S(1)} %multiply_add_fusion) | copy-start | bytes 6916
  11.0 83.3 %all-to-all-start.2 = ((bf16[32,1,18]{2,1,0:T(2,128)(2,1)}), bf16[32,1,18]{2,1,0:T(2,128)(2,1)S(1)}, u32[]{:S(2)}, u32[]{:S(2)}) async-start(bf16[32,1,18]{2,1,0:T(2,128)(2,1)} %all_to_all.52), calls=%async_computation.3 | async-start | bytes 32768 | tf_op jit(solution)/shard_map/all_to_all | solution.py:46
  19.0 36.2 %copy-start.11 = (f32[576]{0:T(1024)}, f32[576]{0:T(1024)S(1)}, u32[]{:S(2)}) copy-start(f32[576]{0:T(1024)S(1)} %convert_reduce_fusion.2) | copy-start | bytes 6916
  19.7 35.5 %copy-start.9 = (s32[576]{0:T(1024)}, s32[576]{0:T(1024)S(1)}, u32[]{:S(2)}) copy-start(s32[576]{0:T(1024)S(1)} %reduce) | copy-start | bytes 6916
  94.3 6.0 copy-start.4
  94.3 6.0 copy-start.5
  94.3 6.1 copy-start.13
  94.3 564.9 %all-to-all-start.3 = ((bf16[32,18,16384]{2,1,0:T(8,128)(2,1)}), bf16[32,18,16384]{2,1,0:T(8,128)(2,1)}, u32[]{:S(2)}, u32[]{:S(2)}) async-start(bf16[32,18,16384]{2,1,0:T(8,128)(2,1)} %reshape.112), calls=%async_computation.4 | async-start | bytes 50331648 | tf_op jit(solution)/shard_map/all_to_all | solution.py:45
  100.3 563.3 %copy-start.6 = (f32[1,1536]{1,0:T(1,128)S(1)}, f32[1,1536]{1,0:T(1,128)}, u32[]{:S(2)}) copy-start(f32[1,1536]{1,0:T(1,128)} %param.18) | copy-start | bytes 18436
  100.3 112.3 %all-gather.3.cloned.1.call-start = ((), (), s32[]{:S(2)}) async-start(), calls=%async_computation.6 | async-start | bytes 3932160 | tf_op jit(solution)/shard_map/all_gather | solution.py:28
  659.2 74.6 %all-to-all-start = ((bf16[128,8,1536]{0,2,1:T(8,128)(2,1)}), bf16[128,8,1536]{0,2,1:T(8,128)(2,1)S(1)}, u32[]{:S(2)}, u32[]{:S(2)}) async-start(bf16[128,8,1536]{0,2,1:T(8,128)(2,1)} %bitcast.96), calls=%async_computation | async-start | bytes 6291456 | tf_op jit(solution)/shard_map/all_to_all | solution.py:32
  662.9 40.6 %all-gather.5.cloned.1.call-start = ((), (), s32[]{:S(2)}) async-start(), calls=%async_computation.7 | async-start | bytes 3932160 | tf_op jit(solution)/shard_map/all_gather | solution.py:29
  694.2 2.2 copy-start
  733.8 1.6 copy-start.1
  735.4 18.5 %slice-start = ((s8[4718592]{0:T(1024)(128)(4,1)}), s8[524288]{0:T(1024)(128)(4,1)S(1)}, s32[]{:S(2)}) async-start(s8[4718592]{0:T(1024)(128)(4,1)} %bitcast.81), calls=%async_computation.9 | async-start | bytes 1048576
  735.4 81.8 %all-to-all-start.1 = ((bf16[128,8,1536]{0,2,1:T(8,128)(2,1)}), bf16[128,8,1536]{0,2,1:T(8,128)(2,1)}, u32[]{:S(2)}, u32[]{:S(2)}) async-start(bf16[128,8,1536]{0,2,1:T(8,128)(2,1)} %bitcast.95), calls=%async_computation.1 | async-start | bytes 6291456 | tf_op jit(solution)/shard_map/all_to_all | solution.py:33
  740.4 13.5 slice-start.1
  817.3 5.7 copy-start.2
  817.3 641.0 %all-to-all-start.4 = ((bf16[32,18,16384]{2,1,0:T(8,128)(2,1)}), bf16[32,18,16384]{2,1,0:T(8,128)(2,1)}, u32[]{:S(2)}, u32[]{:S(2)}) async-start(bf16[32,18,16384]{2,1,0:T(8,128)(2,1)} %reshape.118), calls=%async_computation.5 | async-start | bytes 50331648 | tf_op jit(solution)/shard_map/all_to_all | solution.py:52
  822.9 716.3 %reduce-scatter.2.cloned.1.call-start = ((), (), s32[]{:S(2)}) async-start(), calls=%async_computation.8 | async-start | bytes 7077888 | tf_op jit(solution)/shard_map/reduce_scatter | solution.py:38
  825.9 4.8 copy-start.3
  863.6 0.7 copy-start.8
  863.6 0.7 copy-start.10
  863.6 0.7 copy-start.12
  863.6 0.7 copy-start.15
Sparse Core Ops, SparseCore 0:
  104.5 108.0 all-gather.2
  665.9 29.2 all-gather.4
  863.7 365.7 reduce-scatter.1
where the time goes:
time: 1560 us; the launch traced here: 1550 us
  waiting for transfers between devices  1180 us (76%)
  local copies, waits for them, and re-layouts  187 us (12%)
  matrix products  125 us (8%)
  starting transfers between devices  27.6 us (2%)
    all_to_all x1, waiting for transfers between devices, collect(): lax.all_to_all(answer_tiles, ('row', 'col'), split_axis=0, concat_axis=0,...  592 us
    all_to_all x1, waiting for transfers between devices, deliver(): lax.all_to_all(sent_tiles, ('row', 'col'), split_axis=0, concat_axis=0, t...  447 us
    all_gather x1, waiting for transfers between devices, panel_part(): lax.all_gather(gamma_cols, 'row', axis=1, tiled=True)  108 us
    unnamed x42, local copies, waits for them, and re-layouts  60.9 us
  transfers between devices with their start and end apart: 8, of which 4 were waited for; matrix products, arithmetic and copies ran while one was open for 21% of the time, Pallas kernels for 0%

commit v1 on v0

v1 whole, which is shorter than its diff:
```python
import functools

import jax
import jax.numpy as jnp
from jax import lax
from jax.experimental import pallas as pl
from jax.experimental.pallas import tpu as pltpu
from jax.sharding import PartitionSpec as P

TILE = 128
PH_STATES = 1536
PANEL_DEV = 128
VMEM_BYTES = 56 * 1024 * 1024


def orbit_lookup(pair_ids, occupancy):
    orbit_ids = jnp.arange(occupancy.shape[0], dtype=jnp.int32)
    return jnp.sum(
        jnp.where(pair_ids[:, None] == orbit_ids[None, :], occupancy[None, :], 0.0), axis=1
    )


def panel_part(eta_pairs, gamma_pairs, pair_first, pair_second, occupancy):
    n_row = lax.axis_size("row")
    n_col = lax.axis_size("col")
    factor = 1.0 - orbit_lookup(pair_first, occupancy) - orbit_lookup(pair_second, occupancy)
    columns = jnp.concatenate([gamma_pairs[:, :PANEL_DEV], eta_pairs[:, :PANEL_DEV]], axis=1)
    columns = (factor[:, None] * columns.astype(jnp.float32)).astype(jnp.bfloat16).T
    columns = columns.reshape(2, PANEL_DEV, eta_pairs.shape[0])
    shares = lax.all_to_all(columns, "col", split_axis=2, concat_axis=1, tiled=True)
    ratio = n_col // n_row
    moves = [
        (i * n_col + j, (j % n_row) * n_col + i * ratio + j // n_row)
        for i in range(n_row)
        for j in range(n_col)
    ]
    shares = lax.ppermute(shares, ("row", "col"), moves)
    panels = lax.all_gather(shares, "row", axis=2, tiled=True)
    contract = (((1,), (1,)), ((), ()))
    leading = lax.dot_general(panels[0], eta_pairs, contract, preferred_element_type=jnp.float32)
    trailing = lax.dot_general(panels[1], gamma_pairs, contract, preferred_element_type=jnp.float32)
    return lax.psum_scatter(
        (leading - trailing).astype(jnp.bfloat16), "col", scatter_dimension=0, tiled=True
    )


def gather_kernel(capacity, col_tiles, ids_ref, weights_ref, matrix_ref, out_ref):
    first = pl.program_id(0) * capacity

    def one(k, carry):
        tile = jnp.maximum(ids_ref[first + k], 0)
        rows = pl.ds(pl.multiple_of((tile // col_tiles) * TILE, TILE), TILE)
        cols = pl.ds(pl.multiple_of((tile % col_tiles) * TILE, TILE), TILE)
        scaled = weights_ref[first + k] * matrix_ref[rows, cols].astype(jnp.float32)
        out_ref[0, k] = scaled.astype(jnp.bfloat16)
        return carry

    lax.fori_loop(0, capacity, one, 0, unroll=True)


def gather_tiles(matrix, ids, weights, blocks, capacity):
    smem = pl.BlockSpec(memory_space=pltpu.SMEM)
    return pl.pallas_call(
        functools.partial(gather_kernel, capacity, matrix.shape[1] // TILE),
        grid=(blocks,),
        in_specs=[smem, smem, pl.BlockSpec(matrix.shape, lambda g: (0, 0))],
        out_specs=pl.BlockSpec((1, capacity, TILE, TILE), lambda g: (g, 0, 0, 0)),
        out_shape=jax.ShapeDtypeStruct((blocks, capacity, TILE, TILE), jnp.bfloat16),
        compiler_params=pltpu.CompilerParams(vmem_limit_bytes=VMEM_BYTES),
        cost_estimate=pl.CostEstimate(
            flops=blocks * capacity * TILE * TILE,
            bytes_accessed=2 * (matrix.size + blocks * capacity * TILE * TILE),
            transcendentals=0,
        ),
        name="gather_tiles",
    )(ids, weights, matrix)


def scatter_kernel(capacity, col_tiles, ids_ref, weights_ref, tiles_ref, out_ref, total):
    step = pl.program_id(0)
    first = step * capacity

    @pl.when(step == 0)
    def _():
        total[...] = jnp.zeros_like(total)

    def one(k, carry):
        tile = ids_ref[first + k]

        @pl.when(tile >= 0)
        def _():
            rows = pl.ds(pl.multiple_of((tile // col_tiles) * TILE, TILE), TILE)
            cols = pl.ds(pl.multiple_of((tile % col_tiles) * TILE, TILE), TILE)
            total[rows, cols] += weights_ref[first + k] * tiles_ref[0, k].astype(jnp.float32)

        return carry

    lax.fori_loop(0, capacity, one, 0)

    @pl.when(step == pl.num_programs(0) - 1)
    def _():
        out_ref[...] = total[...].astype(jnp.bfloat16)


def scatter_tiles(tiles, ids, weights, shape):
    blocks, capacity = tiles.shape[:2]
    smem = pl.BlockSpec(memory_space=pltpu.SMEM)
    return pl.pallas_call(
        functools.partial(scatter_kernel, capacity, shape[1] // TILE),
        grid=(blocks,),
        in_specs=[
            smem,
            smem,
            pl.BlockSpec((1, capacity, TILE, TILE), lambda g: (g, 0, 0, 0)),
        ],
        out_specs=pl.BlockSpec(shape, lambda g: (0, 0)),
        out_shape=jax.ShapeDtypeStruct(shape, jnp.bfloat16),
        scratch_shapes=[pltpu.VMEM(shape, jnp.float32)],
        compiler_params=pltpu.CompilerParams(vmem_limit_bytes=VMEM_BYTES),
        cost_estimate=pl.CostEstimate(
            flops=2 * tiles.size,
            bytes_accessed=2 * (tiles.size + shape[0] * shape[1]),
            transcendentals=0,
        ),
        name="scatter_tiles",
    )(ids, weights, tiles)


def exchange(tiles):
    return lax.all_to_all(tiles, ("row", "col"), split_axis=0, concat_axis=0, tiled=True)


def recoupled_part(
    eta_pairs,
    gamma_recoupled,
    ph_factor,
    tile_source,
    tile_owner,
    tile_place,
    sixj_weight,
    live_count,
):
    blocks = lax.axis_size("row") * lax.axis_size("col")
    slot_total = tile_source.shape[1]
    capacity = max(2, (slot_total + blocks - 1) // blocks)
    sources = tile_source[0]
    owners = tile_owner[0]
    places = tile_place[0]
    weights = sixj_weight[0].astype(jnp.float32)
    slot_ids = jnp.arange(slot_total, dtype=jnp.int32)
    is_live = slot_ids < live_count[0]
    same_owner = (
        (owners[:, None] == owners[None, :])
        & is_live[None, :]
        & (slot_ids[None, :] < slot_ids[:, None])
    )
    slot_rank = jnp.sum(same_owner.astype(jnp.int32), axis=1)
    buffer_ids = jnp.arange(blocks * capacity, dtype=jnp.int32)
    slot_buffer = jnp.where(is_live, owners * capacity + slot_rank, -1)
    hit = buffer_ids[:, None] == slot_buffer[None, :]
    buffer_source = jnp.sum(jnp.where(hit, sources[None, :] + 1, 0), axis=1) - 1
    buffer_place = jnp.sum(jnp.where(hit, places[None, :] + 1, 0), axis=1) - 1
    buffer_weight = jnp.sum(jnp.where(hit, weights[None, :], 0.0), axis=1)
    codes = exchange(buffer_place.reshape(blocks, capacity)).reshape(blocks * capacity)
    ones = jnp.ones((blocks * capacity,), jnp.float32)
    sent = gather_tiles(eta_pairs, buffer_source, buffer_weight, blocks, capacity)
    eta_ph = scatter_tiles(exchange(sent), codes, ones, (PH_STATES, PH_STATES))
    gamma_ph = gamma_recoupled[0]
    scale = ph_factor[0]
    gamma_scaled = (scale[:, None] * gamma_ph.astype(jnp.float32)).astype(jnp.bfloat16)
    eta_scaled = (scale[:, None] * eta_ph.astype(jnp.float32)).astype(jnp.bfloat16)
    product = jnp.dot(eta_ph, gamma_scaled, preferred_element_type=jnp.float32)
    product = (product - jnp.dot(gamma_ph, eta_scaled, preferred_element_type=jnp.float32)).astype(
        jnp.bfloat16
    )
    answer = gather_tiles(product, codes, ones, blocks, capacity)
    return scatter_tiles(exchange(answer), buffer_source, buffer_weight, eta_pairs.shape)


def local(
    eta_pairs,
    gamma_pairs,
    pair_first,
    pair_second,
    occupancy,
    gamma_recoupled,
    ph_factor,
    tile_source,
    tile_owner,
    tile_place,
    sixj_weight,
    live_count,
):
    panel_update = panel_part(eta_pairs, gamma_pairs, pair_first, pair_second, occupancy)
    recoupled_update = recoupled_part(
        eta_pairs,
        gamma_recoupled,
        ph_factor,
        tile_source,
        tile_owner,
        tile_place,
        sixj_weight,
        live_count,
    )
    return (panel_update, recoupled_update)


def solution(mesh):
    in_specs = (
        P("row", "col"),
        P("row", "col"),
        P("row"),
        P("row"),
        P(),
        P(("row", "col"), None, None),
        P(("row", "col"), None),
        P(("row", "col"), None),
        P(("row", "col"), None),
        P(("row", "col"), None),
        P(("row", "col"), None),
        P(("row", "col")),
    )
    out_specs = (P("col", "row"), P("row", "col"))
    return jax.shard_map(local, mesh=mesh, in_specs=in_specs, out_specs=out_specs, check_vma=False)
```

time: 1560 us -> 1260 us (0.81)
  local copies, waits for them, and re-layouts: 187 us -> 9.71 us
  waiting for transfers between devices: 1180 us -> 1040 us
  Pallas kernels: 0 us -> 103 us
  matrix products: 125 us -> 58.7 us
    all_to_all x5 -> x4, waiting for transfers between devices: 1070 us -> 414 us  [the longest x3 414 us: exchange(): lax.all_to_all(tiles, ('row', 'col'), split_axis=0, concat_axis=0, tiled=...]
    all_gather x2 -> x1, waiting for transfers between devices: 108 us -> 540 us  [panel_part(): panels = lax.all_gather(shares, 'row', axis=2, tiled=True)]
    pallas_call x0 -> x4, Pallas kernels: none -> 103 us  [the longest x2 65.2 us: scatter_tiles(): pl.pallas_call(functools.partial(scatter_kernel, capacity, shape[1] // TI...]
    reshape x7 -> x2, local copies, waits for them, and re-layouts: 99.8 us -> 3.59 us  [the longest x1 2.9 us: panel_part(): columns = columns.reshape(2, PANEL_DEV, eta_pairs.shape[0])]
    reduce_scatter x1, waiting for transfers between devices: 0.01 us -> 83.6 us  [panel_part(): lax.psum_scatter((leading - trailing).astype(jnp.bfloat16), 'col', scatte...]
    dot_general x9 -> x2, matrix products: 98.7 us -> 33.9 us  [the longest x1 17.8 us: panel_part(): lax.dot_general(panels[0], eta_pairs, contract, preferred_element_type=jn...]
    unnamed x42 -> x18, local copies, waits for them, and re-layouts: 60.9 us -> 1.74 us
    transpose x2 -> x0, local copies, waits for them, and re-layouts: 17.3 us -> none  [the longest x1 13.1 us: recoupled_part(): eta_tiles = eta_pairs.reshape(row_tiles, TILE, col_tiles, TILE).transpose...]
  transfers between devices with their start and end apart: 8 -> 7, of which waited for: 4 -> 3; matrix products, arithmetic and copies ran while one was open for 21% -> 6% of each run, Pallas kernels for 0% -> 8%
where the time goes in v1:
time: 1260 us
  waiting for transfers between devices  1040 us (83%)
  Pallas kernels  103 us (8%)
  matrix products  58.7 us (5%)
  starting transfers between devices  24.5 us (2%)
  between operations  14.9 us (1%)
    all_gather x1, waiting for transfers between devices, panel_part(): panels = lax.all_gather(shares, 'row', axis=2, tiled=True)  540 us
    all_to_all x3, waiting for transfers between devices, exchange(): lax.all_to_all(tiles, ('row', 'col'), split_axis=0, concat_axis=0, tiled=...  414 us
    reduce_scatter x1, waiting for transfers between devices, panel_part(): lax.psum_scatter((leading - trailing).astype(jnp.bfloat16), 'col', scatte...  83.6 us
    pallas_call x2, Pallas kernels, scatter_tiles(): pl.pallas_call(functools.partial(scatter_kernel, capacity, shape[1] // TI...  65.2 us
    pallas_call x2, Pallas kernels, gather_tiles(): pl.pallas_call(functools.partial(gather_kernel, capacity, matrix.shape[1]...  37.8 us
  transfers between devices with their start and end apart: 7, of which 3 were waited for; matrix products, arithmetic and copies ran while one was open for 6% of the time, Pallas kernels for 8%

profile of v1, /device:TPU:0, one launch (start us, length us, event | category | flops | bytes accessed | tf_op | source)
XLA Modules:
  0.0 1255.3 jit_solution(12571620913012731083)
XLA Ops:
  7.8 0.7 add_reduce_fusion.1
  8.5 0.7 reduce
  9.2 0.3 convert_reduce_fusion
  9.5 0.7 fusion.8
  10.3 0.6 select_reduce_fusion.2
  10.9 0.7 sub.37
  11.6 7.3 all-to-all-start.1
  18.9 0.6 broadcast_add_fusion.1.ids_ref
  19.5 0.7 convert_reduce_fusion.1
  20.2 0.8 select_reduce_fusion.3.weights_ref
  21.0 19.6 %gather_tiles.2 = bf16[32,18,128,128]{3,2,1,0:T(8,128)(2,1)} custom-call(s32[576]{0:T(1024)} %broadcast_add_fusion.1.ids_ref, f32[576]{0:T(1024)} %select_reduce_fusion.3.weights_ref, bf16[3072,1536]{1,0:T(8,128)(2,1)} %matrix_ref.1), custom_call_target="tpu_custom_call" | custom-call | flops 9437184 | bytes 28311552 | tf_op jit(solution)/shard_map/gather_tiles/pallas_call | solution.py:63
  40.6 5.9 all-to-all-start.2
  46.6 0.0 slice-start
  46.6 0.0 copy-start.2
  46.6 0.0 copy-start.3
  46.6 0.0 copy-start.5
  46.7 0.0 copy-start.4
  46.7 0.3 copy.38
  47.0 0.8 slice-done
  47.7 0.3 copy.39
  48.1 0.9 select_reduce_fusion.1
  49.0 0.3 multiply_convert_fusion.4
  49.3 2.9 copy.32
  52.3 0.5 broadcast.51
  52.8 0.7 reduce.13
  53.5 0.7 reshape.49.ids_ref
  54.2 413.7 %all-to-all-done.2.tiles_ref = bf16[32,18,128,128]{3,2,1,0:T(8,128)(2,1)} async-done(((bf16[32,18,128,128]{3,2,1,0:T(8,128)(2,1)}), bf16[32,18,128,128]{3,2,1,0:T(8,128)(2,1)}, u32[]{:S(2)}, u32[]{:S(2)}) %all-to-all-start.2) | async-done | bytes 18874400 | tf_op jit(solution)/shard_map/all_to_all | solution.py:130
  467.9 3.6 all-to-all-start
  471.5 0.6 broadcast_in_dim.87.weights_ref
  472.0 30.7 %scatter_tiles.2 = bf16[1536,1536]{1,0:T(8,128)(2,1)} custom-call(s32[576]{0:T(1024)} %reshape.49.ids_ref, f32[576]{0:T(1024)} %broadcast_in_dim.87.weights_ref, bf16[32,18,128,128]{3,2,1,0:T(8,128)(2,1)} %all-to-all-done.2.tiles_ref), custom_call_target="tpu_custom_call" | custom-call | flops 18874368 | bytes 23592960 | tf_op jit(solution)/shard_map/scatter_tiles/pallas_call | solution.py:108
  502.8 13.3 %fusion.1 = f32[1536,1536]{0,1:T(8,128)} fusion(bf16[1536,1536]{1,0:T(8,128)(2,1)} %scatter_tiles.2, bf16[1,1536,1536]{2,1,0:T(8,128)(2,1)} %param.17, f32[1536]{0:T(1024)S(1)} %reduce.6), kind=kOutput, calls=%fused_computation.5 | convolution fusion | flops 7254835200 | bytes 18880512 | tf_op jit(solution)/shard_map/dot_general | solution.py:173
  516.1 11.5 fusion.matrix_ref
  527.6 18.2 %gather_tiles.3 = bf16[32,18,128,128]{3,2,1,0:T(8,128)(2,1)} custom-call(s32[576]{0:T(1024)} %reshape.49.ids_ref, f32[576]{0:T(1024)} %broadcast_in_dim.87.weights_ref, bf16[1536,1536]{1,0:T(8,128)(2,1)} %fusion.matrix_ref), custom_call_target="tpu_custom_call" | custom-call | flops 9437184 | bytes 23592960 | tf_op jit(solution)/shard_map/gather_tiles/pallas_call | solution.py:63
  545.8 5.3 all-to-all-start.3
  551.2 0.2 all-gather.2.cloned.1.call-start
  551.4 0.2 copy.33
  551.6 1.6 copy.34
  553.2 2.1 collective-permute-start
  555.2 1.1 copy-done.1
  556.4 0.0 all-gather.2.cloned.1.call-update
  556.4 0.0 reduce-scatter.2.cloned.1.call-start
  556.5 540.0 %all-gather.2.cloned.1.call-done = bf16[2,1024,1536]{2,1,0:T(8,128)(2,1)} async-done(((bf16[2,1024,384]{2,1,0:T(8,128)(2,1)}), bf16[2,1024,1536]{2,1,0:T(8,128)(2,1)}) %all-gather.2.cloned.1.call-update) | async-done | bytes 6291472 | tf_op jit(solution)/shard_map/all_gather | solution.py:38
  1096.5 16.1 %fusion.6 = f32[1024,3072]{1,0:T(8,128)} fusion(bf16[3072,1536]{1,0:T(8,128)(2,1)} %param.13, bf16[2,1024,1536]{2,1,0:T(8,128)(2,1)} %all-gather.2.cloned.1.call-done), kind=kOutput, calls=%fused_computation.11 | convolution fusion | flops 9663676416 | bytes 25165824 | tf_op jit(solution)/shard_map/dot_general | solution.py:41
  1112.6 17.8 %subtract_convert_fusion = bf16[1024,3072]{1,0:T(8,128)(2,1)} fusion(f32[1024,3072]{1,0:T(8,128)} %fusion.6, bf16[3072,1536]{1,0:T(8,128)(2,1)} %matrix_ref.1, bf16[2,1024,1536]{2,1,0:T(8,128)(2,1)} %all-gather.2.cloned.1.call-done), kind=kOutput, calls=%fused_computation | convolution fusion | flops 9669967872 | bytes 31457280 | tf_op jit(solution)/shard_map/dot_general | solution.py:40
  1130.3 0.0 reduce-scatter.2.cloned.1.call-update
  1130.4 0.0 all-to-all-done.3.tiles_ref
  1130.4 34.5 %scatter_tiles.3 = bf16[3072,1536]{1,0:T(8,128)(2,1)} custom-call(s32[576]{0:T(1024)} %broadcast_add_fusion.1.ids_ref, f32[576]{0:T(1024)} %select_reduce_fusion.3.weights_ref, bf16[32,18,128,128]{3,2,1,0:T(8,128)(2,1)} %all-to-all-done.3.tiles_ref), custom_call_target="tpu_custom_call" | custom-call | flops 18874368 | bytes 28311552 | tf_op jit(solution)/shard_map/scatter_tiles/pallas_call | solution.py:108
  1164.9 83.6 %reduce-scatter.2.cloned.1.call-done = bf16[128,3072]{1,0:T(8,128)(2,1)} async-done(((bf16[1024,3072]{1,0:T(8,128)(2,1)}), bf16[128,3072]{1,0:T(8,128)(2,1)}) %reduce-scatter.2.cloned.1.call-update) | async-done | bytes 786448 | tf_op jit(solution)/shard_map/reduce_scatter | solution.py:42
  (21 shorter events, 0.1 us)
Async XLA Ops:
  11.6 29.1 %all-to-all-start.1 = ((s32[32,1,18]{2,1,0:T(1,128)}), s32[32,1,18]{2,1,0:T(1,128)S(1)}, u32[]{:S(2)}, u32[]{:S(2)}) async-start(s32[32,1,18]{2,1,0:T(1,128)} %bitcast.8), calls=%async_computation.2 | async-start | bytes 32768 | tf_op jit(solution)/shard_map/all_to_all | solution.py:130
  40.6 6.0 slice-start.1
  40.6 427.2 %all-to-all-start.2 = ((bf16[32,18,128,128]{3,2,1,0:T(8,128)(2,1)}), bf16[32,18,128,128]{3,2,1,0:T(8,128)(2,1)}, u32[]{:S(2)}, u32[]{:S(2)}) async-start(bf16[32,18,128,128]{3,2,1,0:T(8,128)(2,1)} %gather_tiles.2), calls=%async_computation.3 | async-start | bytes 37748736 | tf_op jit(solution)/shard_map/all_to_all | solution.py:130
  46.6 1.1 slice-start
  46.6 1.4 copy-start.2
  46.6 1.4 copy-start.3
  46.6 1.4 copy-start.5
  46.7 5.6 copy-start.4
  467.9 78.0 %all-to-all-start = ((bf16[2,128,3072]{1,0,2:T(2,128)(2,1)}), bf16[2,128,3072]{1,0,2:T(2,128)(2,1)S(1)}, u32[]{:S(2)}, u32[]{:S(2)}) async-start(bf16[2,128,3072]{1,0,2:T(2,128)(2,1)} %copy.32), calls=%async_computation | async-start | bytes 3145728 | tf_op jit(solution)/shard_map/all_to_all | solution.py:30
  472.0 44.1 %slice-start.2 = ((s8[4718592]{0:T(1024)(128)(4,1)}), s8[524288]{0:T(1024)(128)(4,1)S(1)}, s32[]{:S(2)}) async-start(s8[4718592]{0:T(1024)(128)(4,1)} %bitcast.34), calls=%async_computation.9 | async-start | bytes 1048576
  502.8 13.3 %copy-start = (bf16[1536,1536]{1,0:T(8,128)(2,1)S(1)}, bf16[1536,1536]{1,0:T(8,128)(2,1)}, u32[]{:S(2)}) copy-start(bf16[1536,1536]{1,0:T(8,128)(2,1)} %scatter_tiles.2) | copy-start | bytes 14155780
  502.8 13.3 %slice-start.3 = ((s8[4718592]{0:T(1024)(128)(4,1)}), s8[4194304]{0:T(1024)(128)(4,1)S(1)}, s32[]{:S(2)}) async-start(s8[4718592]{0:T(1024)(128)(4,1)} %bitcast.34), calls=%async_computation.10 | async-start | bytes 8388608
  545.8 584.6 %all-to-all-start.3 = ((bf16[32,18,128,128]{3,2,1,0:T(8,128)(2,1)}), bf16[32,18,128,128]{3,2,1,0:T(8,128)(2,1)}, u32[]{:S(2)}, u32[]{:S(2)}) async-start(bf16[32,18,128,128]{3,2,1,0:T(8,128)(2,1)} %gather_tiles.3), calls=%async_computation.4 | async-start | bytes 37748736 | tf_op jit(solution)/shard_map/all_to_all | solution.py:130
  551.2 545.3 %all-gather.2.cloned.1.call-start = ((), (), s32[]{:S(2)}) async-start(), calls=%async_computation.5 | async-start | bytes 7864320 | tf_op jit(solution)/shard_map/all_gather | solution.py:38
  553.2 2.1 collective-permute-start
  555.2 1.1 copy-start.1
  556.4 692.1 %reduce-scatter.2.cloned.1.call-start = ((), (), s32[]{:S(2)}) async-start(), calls=%async_computation.6 | async-start | bytes 7077888 | tf_op jit(solution)/shard_map/reduce_scatter | solution.py:42
Sparse Core Ops, SparseCore 0:
  556.5 539.8 all-gather.1
  1130.5 117.9 reduce-scatter.1

commit v2 on v1

--- a/solution.py
+++ b/solution.py
@@ -20,14 +20,17 @@
     )
 
 
-def panel_part(eta_pairs, gamma_pairs, pair_first, pair_second, occupancy):
-    n_row = lax.axis_size("row")
-    n_col = lax.axis_size("col")
+def panel_shares(eta_pairs, gamma_pairs, pair_first, pair_second, occupancy):
     factor = 1.0 - orbit_lookup(pair_first, occupancy) - orbit_lookup(pair_second, occupancy)
     columns = jnp.concatenate([gamma_pairs[:, :PANEL_DEV], eta_pairs[:, :PANEL_DEV]], axis=1)
     columns = (factor[:, None] * columns.astype(jnp.float32)).astype(jnp.bfloat16).T
     columns = columns.reshape(2, PANEL_DEV, eta_pairs.shape[0])
-    shares = lax.all_to_all(columns, "col", split_axis=2, concat_axis=1, tiled=True)
+    return lax.all_to_all(columns, "col", split_axis=2, concat_axis=1, tiled=True)
+
+
+def panel_gather(shares):
+    n_row = lax.axis_size("row")
+    n_col = lax.axis_size("col")
     ratio = n_col // n_row
     moves = [
         (i * n_col + j, (j % n_row) * n_col + i * ratio + j // n_row)
@@ -35,7 +38,10 @@
         for j in range(n_col)
     ]
     shares = lax.ppermute(shares, ("row", "col"), moves)
-    panels = lax.all_gather(shares, "row", axis=2, tiled=True)
+    return lax.all_gather(shares, "row", axis=2, tiled=True)
+
+
+def panel_product(panels, eta_pairs, gamma_pairs):
     contract = (((1,), (1,)), ((), ()))
     leading = lax.dot_general(panels[0], eta_pairs, contract, preferred_element_type=jnp.float32)
     trailing = lax.dot_general(panels[1], gamma_pairs, contract, preferred_element_type=jnp.float32)
@@ -76,61 +82,93 @@
     )(ids, weights, matrix)
 
 
-def scatter_kernel(capacity, col_tiles, ids_ref, weights_ref, tiles_ref, out_ref, total):
+def scatter_kernel(capacity, col_tiles, ids_ref, weights_ref, *refs):
+    tiles_refs, out_ref, total = refs[:-2], refs[-2], refs[-1]
     step = pl.program_id(0)
     first = step * capacity
+    part_steps = pl.num_programs(0) // len(tiles_refs)
 
     @pl.when(step == 0)
     def _():
         total[...] = jnp.zeros_like(total)
 
-    def one(k, carry):
-        tile = ids_ref[first + k]
-
-        @pl.when(tile >= 0)
-        def _():
-            rows = pl.ds(pl.multiple_of((tile // col_tiles) * TILE, TILE), TILE)
-            cols = pl.ds(pl.multiple_of((tile % col_tiles) * TILE, TILE), TILE)
-            total[rows, cols] += weights_ref[first + k] * tiles_ref[0, k].astype(jnp.float32)
-
-        return carry
-
-    lax.fori_loop(0, capacity, one, 0)
+    def add_block(tiles_ref):
+        def one(k, carry):
+            tile = ids_ref[first + k]
+
+            @pl.when(tile >= 0)
+            def _():
+                rows = pl.ds(pl.multiple_of((tile // col_tiles) * TILE, TILE), TILE)
+                cols = pl.ds(pl.multiple_of((tile % col_tiles) * TILE, TILE), TILE)
+                total[rows, cols] += weights_ref[first + k] * tiles_ref[0, k].astype(jnp.float32)
+
+            return carry
+
+        lax.fori_loop(0, capacity, one, 0)
+
+    for part, tiles_ref in enumerate(tiles_refs):
+        pl.when(step // part_steps == part)(functools.partial(add_block, tiles_ref))
 
     @pl.when(step == pl.num_programs(0) - 1)
     def _():
         out_ref[...] = total[...].astype(jnp.bfloat16)
 
 
-def scatter_tiles(tiles, ids, weights, shape):
-    blocks, capacity = tiles.shape[:2]
+def part_spec(part, blocks, capacity):
+    return pl.BlockSpec(
+        (1, capacity, TILE, TILE),
+        lambda g: (jnp.clip(g - part * blocks, 0, blocks - 1), 0, 0, 0),
+    )
+
+
+def scatter_tiles(parts, ids, weights, shape):
+    blocks, capacity = parts[0].shape[:2]
     smem = pl.BlockSpec(memory_space=pltpu.SMEM)
+    size = len(parts) * parts[0].size
     return pl.pallas_call(
         functools.partial(scatter_kernel, capacity, shape[1] // TILE),
-        grid=(blocks,),
-        in_specs=[
-            smem,
-            smem,
-            pl.BlockSpec((1, capacity, TILE, TILE), lambda g: (g, 0, 0, 0)),
-        ],
+        grid=(len(parts) * blocks,),
+        in_specs=[smem, smem] + [part_spec(p, blocks, capacity) for p in range(len(parts))],
         out_specs=pl.BlockSpec(shape, lambda g: (0, 0)),
         out_shape=jax.ShapeDtypeStruct(shape, jnp.bfloat16),
         scratch_shapes=[pltpu.VMEM(shape, jnp.float32)],
         compiler_params=pltpu.CompilerParams(vmem_limit_bytes=VMEM_BYTES),
         cost_estimate=pl.CostEstimate(
-            flops=2 * tiles.size,
-            bytes_accessed=2 * (tiles.size + shape[0] * shape[1]),
+            flops=2 * size,
+            bytes_accessed=2 * (size + shape[0] * shape[1]),
             transcendentals=0,
         ),
         name="scatter_tiles",
-    )(ids, weights, tiles)
-
-
-def exchange(tiles):
-    return lax.all_to_all(tiles, ("row", "col"), split_axis=0, concat_axis=0, tiled=True)
+    )(ids, weights, *parts)
+
+
+def half_groups():
+    n_row = lax.axis_size("row")
+    n_col = lax.axis_size("col")
+    half = n_col // 2
+    return [
+        [i * n_col + h * half + j for i in range(n_row) for j in range(half)] for h in range(2)
+    ]
+
+
+def exchange(tiles, axis=0):
+    return lax.all_to_all(
+        tiles,
+        ("row", "col"),
+        split_axis=axis,
+        concat_axis=axis,
+        axis_index_groups=half_groups(),
+        tiled=True,
+    )
+
+
+def mirror(matrix):
+    n_col = lax.axis_size("col")
+    return lax.ppermute(matrix, "col", [(j, (j + n_col // 2) % n_col) for j in range(n_col)])
 
 
 def recoupled_part(
+    shares,
     eta_pairs,
     gamma_recoupled,
     ph_factor,
@@ -140,7 +178,10 @@
     sixj_weight,
     live_count,
 ):
-    blocks = lax.axis_size("row") * lax.axis_size("col")
+    n_col = lax.axis_size("col")
+    blocks = lax.axis_size("row") * n_col
+    near = blocks // 2
+    half = n_col // 2
     slot_total = tile_source.shape[1]
     capacity = max(2, (slot_total + blocks - 1) // blocks)
     sources = tile_source[0]
@@ -156,15 +197,32 @@
     )
     slot_rank = jnp.sum(same_owner.astype(jnp.int32), axis=1)
     buffer_ids = jnp.arange(blocks * capacity, dtype=jnp.int32)
-    slot_buffer = jnp.where(is_live, owners * capacity + slot_rank, -1)
+    owner_col = owners % n_col
+    is_far = (owner_col // half != lax.axis_index("col") // half).astype(jnp.int32)
+    owner_at = is_far * near + (owners // n_col) * half + owner_col % half
+    slot_buffer = jnp.where(is_live, owner_at * capacity + slot_rank, -1)
     hit = buffer_ids[:, None] == slot_buffer[None, :]
     buffer_source = jnp.sum(jnp.where(hit, sources[None, :] + 1, 0), axis=1) - 1
     buffer_place = jnp.sum(jnp.where(hit, places[None, :] + 1, 0), axis=1) - 1
     buffer_weight = jnp.sum(jnp.where(hit, weights[None, :], 0.0), axis=1)
-    codes = exchange(buffer_place.reshape(blocks, capacity)).reshape(blocks * capacity)
-    ones = jnp.ones((blocks * capacity,), jnp.float32)
-    sent = gather_tiles(eta_pairs, buffer_source, buffer_weight, blocks, capacity)
-    eta_ph = scatter_tiles(exchange(sent), codes, ones, (PH_STATES, PH_STATES))
+    codes = exchange(buffer_place.reshape(2, near, capacity), 1).reshape(2, near * capacity)
+    near_codes, far_codes = codes[0], codes[1]
+    split = near * capacity
+    ones = jnp.ones((split,), jnp.float32)
+    ph_shape = (PH_STATES, PH_STATES)
+    far_sent = gather_tiles(
+        eta_pairs, buffer_source[split:], buffer_weight[split:], near, capacity
+    )
+    far_sum = scatter_tiles([exchange(far_sent)], far_codes, ones, ph_shape)
+    near_weight, shares, far_sum = lax.optimization_barrier(
+        (buffer_weight[:split], shares, far_sum)
+    )
+    moved = mirror(far_sum)
+    near_sent = gather_tiles(eta_pairs, buffer_source[:split], near_weight, near, capacity)
+    near_sum = scatter_tiles([exchange(near_sent)], near_codes, ones, ph_shape)
+    panels = panel_gather(shares)
+    moved, panels = lax.optimization_barrier((moved, panels))
+    eta_ph = (near_sum.astype(jnp.float32) + moved.astype(jnp.float32)).astype(jnp.bfloat16)
     gamma_ph = gamma_recoupled[0]
     scale = ph_factor[0]
     gamma_scaled = (scale[:, None] * gamma_ph.astype(jnp.float32)).astype(jnp.bfloat16)
@@ -173,8 +231,13 @@
     product = (product - jnp.dot(gamma_ph, eta_scaled, preferred_element_type=jnp.float32)).astype(
         jnp.bfloat16
     )
-    answer = gather_tiles(product, codes, ones, blocks, capacity)
-    return scatter_tiles(exchange(answer), buffer_source, buffer_weight, eta_pairs.shape)
+    moved_product = mirror(product)
+    near_back = exchange(gather_tiles(product, near_codes, ones, near, capacity))
+    far_back = exchange(gather_tiles(moved_product, far_codes, ones, near, capacity))
+    update = scatter_tiles(
+        [near_back, far_back], buffer_source, buffer_weight, eta_pairs.shape
+    )
+    return panels, update
 
 
 def local(
@@ -191,8 +254,9 @@
     sixj_weight,
     live_count,
 ):
-    panel_update = panel_part(eta_pairs, gamma_pairs, pair_first, pair_second, occupancy)
-    recoupled_update = recoupled_part(
+    shares = panel_shares(eta_pairs, gamma_pairs, pair_first, pair_second, occupancy)
+    panels, recoupled_update = recoupled_part(
+        shares,
         eta_pairs,
         gamma_recoupled,
         ph_factor,
@@ -202,6 +266,7 @@
         sixj_weight,
         live_count,
     )
+    panel_update = panel_product(panels, eta_pairs, gamma_pairs)
     return (panel_update, recoupled_update)
 
 

time: 1260 us -> 1120 us (0.89)
  waiting for transfers between devices: 1040 us -> 711 us
  starting transfers between devices: 24.5 us -> 198 us
    all_gather x1, waiting for transfers between devices: 540 us -> 0.01 us  [panel_gather(): return lax.all_gather(shares, 'row', axis=2, tiled=True)]
    ppermute x1 -> x3, waiting for transfers between devices: 0.01 us -> 411 us  [the longest x2 411 us: mirror(): lax.ppermute(matrix, 'col', [(j, (j + n_col // 2) % n_col) for j in range...]
    all_to_all x4 -> x6, waiting for transfers between devices: 414 us -> 251 us  [the longest x5 227 us: exchange(): lax.all_to_all(tiles, ('row', 'col'), split_axis=axis, concat_axis=axis,...]
    ppermute x1 -> x3, starting transfers between devices: 2.06 us -> 144 us  [the longest x2 143 us: mirror(): lax.ppermute(matrix, 'col', [(j, (j + n_col // 2) % n_col) for j in range...]
    reduce_scatter x1, waiting for transfers between devices: 83.6 us -> 49.3 us  [panel_product(): lax.psum_scatter((leading - trailing).astype(jnp.bfloat16), 'col', scatte...]
    all_to_all x4 -> x6, starting transfers between devices: 22.2 us -> 53.4 us  [the longest x5 47.2 us: exchange(): lax.all_to_all(tiles, ('row', 'col'), split_axis=axis, concat_axis=axis,...]
    pallas_call x2 -> x4, Pallas kernels: 37.8 us -> 43.8 us  [gather_tiles(): pl.pallas_call(functools.partial(gather_kernel, capacity, matrix.shape[1]...]
    pallas_call x2 -> x3, Pallas kernels: 65.2 us -> 68.2 us  [scatter_tiles(): pl.pallas_call(functools.partial(scatter_kernel, capacity, shape[1] // TI...]
  transfers between devices with their start and end apart: 7 -> 11, of which waited for: 3 -> 6; matrix products, arithmetic and copies ran while one was open for 6% -> 4% of each run, Pallas kernels for 8% -> 5%
where the time goes in v2:
time: 1120 us
  waiting for transfers between devices  711 us (63%)
  starting transfers between devices  198 us (18%)
  Pallas kernels  112 us (10%)
  matrix products  60.8 us (5%)
  between operations  15 us (1%)
  local copies, waits for them, and re-layouts  13 us (1%)
    ppermute x2, waiting for transfers between devices, mirror(): lax.ppermute(matrix, 'col', [(j, (j + n_col // 2) % n_col) for j in range...  411 us
    all_to_all x5, waiting for transfers between devices, exchange(): lax.all_to_all(tiles, ('row', 'col'), split_axis=axis, concat_axis=axis,...  227 us
    ppermute x2, starting transfers between devices, mirror(): lax.ppermute(matrix, 'col', [(j, (j + n_col // 2) % n_col) for j in range...  143 us
    pallas_call x3, Pallas kernels, scatter_tiles(): pl.pallas_call(functools.partial(scatter_kernel, capacity, shape[1] // TI...  68.2 us
    reduce_scatter x1, waiting for transfers between devices, panel_product(): lax.psum_scatter((leading - trailing).astype(jnp.bfloat16), 'col', scatte...  49.3 us
    all_to_all x5, starting transfers between devices, exchange(): lax.all_to_all(tiles, ('row', 'col'), split_axis=axis, concat_axis=axis,...  47.2 us
    pallas_call x4, Pallas kernels, gather_tiles(): pl.pallas_call(functools.partial(gather_kernel, capacity, matrix.shape[1]...  43.8 us
    all_to_all x1, waiting for transfers between devices, panel_shares(): lax.all_to_all(columns, 'col', split_axis=2, concat_axis=1, tiled=True)  24.1 us
  transfers between devices with their start and end apart: 11, of which 6 were waited for; matrix products, arithmetic and copies ran while one was open for 4% of the time, Pallas kernels for 5%

profile of v2, /device:TPU:0, one launch (start us, length us, event | category | flops | bytes accessed | tf_op | source)
XLA Modules:
  0.0 1115.5 jit_solution(9301095006883039311)
XLA Ops:
  7.2 0.8 reduce
  8.6 0.7 add_reduce_fusion
  9.3 0.7 add_reduce_fusion.1
  10.1 0.3 convert_reduce_fusion
  10.4 0.7 fusion.13
  11.1 0.6 select_reduce_fusion.2
  11.8 0.6 copy.41
  12.5 6.3 all-to-all-start.1
  18.8 1.2 slice.34
  19.9 0.3 copy.45
  20.2 0.3 copy.44
  20.6 0.9 select_reduce_fusion.1
  21.5 0.3 multiply_convert_fusion.4
  21.8 2.9 copy.38
  24.7 6.1 all-to-all-start
  31.2 0.6 fusion.16
  31.8 0.7 fusion.15
  32.5 11.6 %gather_tiles.4 = bf16[16,18,128,128]{3,2,1,0:T(8,128)(2,1)} custom-call(s32[288]{0:T(512)} %get-tuple-element.19.ids_ref, f32[288]{0:T(512)} %get-tuple-element.20.weights_ref, bf16[3072,1536]{1,0:T(8,128)(2,1)} %matrix_ref.3), custom_call_target="tpu_custom_call" | custom-call | flops 4718592 | bytes 18874368 | tf_op jit(solution)/shard_map/gather_tiles/pallas_call | solution.py:69
  44.0 24.1 %all-to-all-done = bf16[2,128,3072]{1,0,2:T(2,128)(2,1)S(1)} async-done(((bf16[2,128,3072]{1,0,2:T(2,128)(2,1)}), bf16[2,128,3072]{1,0,2:T(2,128)(2,1)S(1)}, u32[]{:S(2)}, u32[]{:S(2)}) %all-to-all-start) | async-done | bytes 1572896 | tf_op jit(solution)/shard_map/all_to_all | solution.py:28
  68.2 4.8 all-to-all-start.2
  73.0 0.6 squeeze.21.ids_ref
  73.8 0.9 copy.40
  74.7 119.2 %all-to-all-done.2.refs_0_ = bf16[16,18,128,128]{3,2,1,0:T(8,128)(2,1)} async-done(((bf16[16,18,128,128]{3,2,1,0:T(8,128)(2,1)}), bf16[16,18,128,128]{3,2,1,0:T(8,128)(2,1)}, u32[]{:S(2)}, u32[]{:S(2)}) %all-to-all-start.2) | async-done | bytes 9437216 | tf_op jit(solution)/shard_map/all_to_all | solution.py:155
  193.9 0.6 broadcast_in_dim.82.weights_ref
  194.5 17.3 %scatter_tiles.3 = bf16[1536,1536]{1,0:T(8,128)(2,1)} custom-call(s32[288]{0:T(512)} %squeeze.21.ids_ref, f32[288]{0:T(512)} %broadcast_in_dim.82.weights_ref, bf16[16,18,128,128]{3,2,1,0:T(8,128)(2,1)} %all-to-all-done.2.refs_0_), custom_call_target="tpu_custom_call" | custom-call | flops 9437184 | bytes 14155776 | tf_op jit(solution)/shard_map/scatter_tiles/pallas_call | solution.py:128
  211.8 11.6 %gather_tiles.5 = bf16[16,18,128,128]{3,2,1,0:T(8,128)(2,1)} custom-call(s32[288]{0:T(512)} %get-tuple-element.18.ids_ref, f32[288]{0:T(512)} %get-tuple-element.10.weights_ref, bf16[3072,1536]{1,0:T(8,128)(2,1)} %matrix_ref.3), custom_call_target="tpu_custom_call" | custom-call | flops 4718592 | bytes 18874368 | tf_op jit(solution)/shard_map/gather_tiles/pallas_call | solution.py:69
  223.4 4.9 all-to-all-start.3
  228.4 0.9 collective-permute-start.1
  229.4 1.2 copy-done.2
  230.5 139.9 %collective-permute-start = (bf16[1536,1536]{1,0:T(8,128)(2,1)}, bf16[1536,1536]{1,0:T(8,128)(2,1)}, u32[]{:S(2)}, u32[]{:S(2)}) collective-permute-start(bf16[1536,1536]{1,0:T(8,128)(2,1)} %scatter_tiles.3), channel_id=1, source_target_pairs={{0,4},{1,5},{2,6},{3,7},{4,0},{5,1},{6,2},{7,3},{8,12},{9,13},{10,... | collective-permute-start | bytes 14155784 | tf_op jit(solution)/shard_map/ppermute | solution.py:167
  370.5 0.7 squeeze.24.ids_ref
  371.2 209.6 %collective-permute-done = bf16[1536,1536]{1,0:T(8,128)(2,1)} collective-permute-done((bf16[1536,1536]{1,0:T(8,128)(2,1)}, bf16[1536,1536]{1,0:T(8,128)(2,1)}, u32[]{:S(2)}, u32[]{:S(2)}) %collective-permute-start) | collective-permute-done | bytes 4718624 | tf_op jit(solution)/shard_map/ppermute | solution.py:167
  580.7 17.3 %scatter_tiles.4 = bf16[1536,1536]{1,0:T(8,128)(2,1)} custom-call(s32[288]{0:T(512)} %squeeze.24.ids_ref, f32[288]{0:T(512)} %broadcast_in_dim.82.weights_ref, bf16[16,18,128,128]{3,2,1,0:T(8,128)(2,1)} %all-to-all-done.3.refs_0_), custom_call_target="tpu_custom_call" | custom-call | flops 9437184 | bytes 14155776 | tf_op jit(solution)/shard_map/scatter_tiles/pallas_call | solution.py:128
  598.0 14.1 %fusion.1 = f32[1536,1536]{0,1:T(8,128)} fusion(bf16[1,1536,1536]{2,1,0:T(8,128)(2,1)} %param.17, f32[1536]{0:T(1024)S(1)} %reduce.7, bf16[1536,1536]{1,0:T(8,128)(2,1)} %collective-permute-done, bf16[1536,1536]{1,0:T(8,128)(2,1)} %scatter_tiles.4), kind=kOutput, calls=%fused_computation.6 | convolution fusion | flops 7264272384 | bytes 23599104 | tf_op jit(solution)/shard_map/dot_general | solution.py:231
  612.2 12.8 %fusion.matrix_ref = bf16[1536,1536]{1,0:T(8,128)(2,1)} fusion(f32[1536,1536]{0,1:T(8,128)} %fusion.1, bf16[1,1536,1536]{2,1,0:T(8,128)(2,1)S(1)} %bitcast.33, f32[1536]{0:T(1024)S(1)} %reduce.7, bf16[1536,1536]{1,0:T(8,128)(2,1)} %collective-permute-done, bf16[1536,1536]{1,0:T(8,128)(2,1)S(1)} %copy-done.1), kind=kOutput, calls=%fused_computation.2 | convolution fusion | flops 7268990976 | bytes 28317696 | tf_op jit(solution)/shard_map/dot_general | solution.py:230
  625.0 10.2 gather_tiles.6
  635.2 11.9 %all-to-all-start.4 = ((bf16[16,18,128,128]{3,2,1,0:T(8,128)(2,1)}), bf16[16,18,128,128]{3,2,1,0:T(8,128)(2,1)}, u32[]{:S(2)}, u32[]{:S(2)}) async-start(bf16[16,18,128,128]{3,2,1,0:T(8,128)(2,1)} %gather_tiles.6), calls=%async_computation.5 | async-start | bytes 18874368 | tf_op jit(solution)/shard_map/all_to_all | solution.py:155
  647.1 3.4 collective-permute-start.2
  650.5 201.2 %collective-permute-done.2.matrix_ref = bf16[1536,1536]{1,0:T(8,128)(2,1)S(1)} collective-permute-done((bf16[1536,1536]{1,0:T(8,128)(2,1)}, bf16[1536,1536]{1,0:T(8,128)(2,1)S(1)}, u32[]{:S(2)}, u32[]{:S(2)}) %collective-permute-start.2) | collective-permute-done | bytes 4718624 | tf_op jit(solution)/shard_map/ppermute | solution.py:167
  851.6 2.2 copy-done
  853.8 10.4 gather_tiles.7
  864.2 19.4 %all-to-all-start.5 = ((bf16[16,18,128,128]{3,2,1,0:T(8,128)(2,1)}), bf16[16,18,128,128]{3,2,1,0:T(8,128)(2,1)}, u32[]{:S(2)}, u32[]{:S(2)}) async-start(bf16[16,18,128,128]{3,2,1,0:T(8,128)(2,1)} %gather_tiles.7), calls=%async_computation.6 | async-start | bytes 18874368 | tf_op jit(solution)/shard_map/all_to_all | solution.py:155
  883.6 0.3 reduce-scatter.2.cloned.1.call-start
  883.9 16.1 %fusion.7 = f32[1024,3072]{1,0:T(8,128)} fusion(bf16[3072,1536]{1,0:T(8,128)(2,1)} %matrix_ref.3, bf16[2,1024,1536]{2,1,0:T(8,128)(2,1)} %all-gather.2.cloned.1.call-done), kind=kOutput, calls=%fused_computation.12 | convolution fusion | flops 9663676416 | bytes 25165824 | tf_op jit(solution)/shard_map/dot_general | solution.py:46
  900.0 17.7 %subtract_convert_fusion = bf16[1024,3072]{1,0:T(8,128)(2,1)} fusion(f32[1024,3072]{1,0:T(8,128)} %fusion.7, bf16[3072,1536]{1,0:T(8,128)(2,1)} %param.13, bf16[2,1024,1536]{2,1,0:T(8,128)(2,1)} %all-gather.2.cloned.1.call-done), kind=kOutput, calls=%fused_computation | convolution fusion | flops 9669967872 | bytes 31457280 | tf_op jit(solution)/shard_map/dot_general | solution.py:47
  917.8 108.0 %all-to-all-done.5.refs_1_ = bf16[16,18,128,128]{3,2,1,0:T(8,128)(2,1)} async-done(((bf16[16,18,128,128]{3,2,1,0:T(8,128)(2,1)}), bf16[16,18,128,128]{3,2,1,0:T(8,128)(2,1)}, u32[]{:S(2)}, u32[]{:S(2)}) %all-to-all-start.5) | async-done | bytes 9437216 | tf_op jit(solution)/shard_map/all_to_all | solution.py:155
  1025.8 33.6 %scatter_tiles.5 = bf16[3072,1536]{1,0:T(8,128)(2,1)} custom-call(s32[576]{0:T(1024)} %copy-done.4, f32[576]{0:T(1024)} %copy-done.3, bf16[16,18,128,128]{3,2,1,0:T(8,128)(2,1)} %all-to-all-done.4.refs_0_, bf16[16,18,128,128]{3,2,1,0:T(8,128)(2,1)} %all-to-all-done.5.refs_1_), custom_call_target="tpu_custom_call" | custom-call | flops 18874368 | bytes 28311552 | tf_op jit(solution)/shard_map/scatter_tiles/pallas_call | solution.py:128
  1059.4 49.3 %reduce-scatter.2.cloned.1.call-done = bf16[128,3072]{1,0:T(8,128)(2,1)} async-done(((bf16[1024,3072]{1,0:T(8,128)(2,1)}), bf16[128,3072]{1,0:T(8,128)(2,1)}) %reduce-scatter.2.cloned.1.call-update) | async-done | bytes 786448 | tf_op jit(solution)/shard_map/reduce_scatter | solution.py:48
  (42 shorter events, 0.8 us)
Async XLA Ops:
  7.2 13.1 %slice-start = ((bf16[3072,1536]{1,0:T(8,128)(2,1)}), bf16[3072,128]{1,0:T(8,128)(2,1)S(1)}, s32[]{:S(2)}) async-start(bf16[3072,1536]{1,0:T(8,128)(2,1)} %param.13), calls=%async_computation.9 | async-start | bytes 1572864 | tf_op jit(solution)/shard_map/slice | solution.py:25
  7.2 13.4 %copy-start.9 = (f32[240]{0:T(256)S(1)}, f32[240]{0:T(256)}, u32[]{:S(2)}) copy-start(f32[240]{0:T(256)} %param.16) | copy-start | bytes 2884
  7.2 13.4 %copy-start.5 = (s32[3072]{0:T(1024)S(1)}, s32[3072]{0:T(1024)}, u32[]{:S(2)}) copy-start(s32[3072]{0:T(1024)} %param.14) | copy-start | bytes 36868
  7.2 13.4 %copy-start.6 = (s32[3072]{0:T(1024)S(1)}, s32[3072]{0:T(1024)}, u32[]{:S(2)}) copy-start(s32[3072]{0:T(1024)} %param.15) | copy-start | bytes 36868
  11.7 20.1 %copy-start.4 = (s32[576]{0:T(1024)}, s32[576]{0:T(1024)S(1)}, u32[]{:S(2)}) copy-start(s32[576]{0:T(1024)S(1)} %get-tuple-element.22.ids_ref) | copy-start | bytes 6916
  12.5 12.3 %all-to-all-start.1 = ((s32[2,16,18]{2,0,1:T(2,128)}), s32[2,16,18]{2,0,1:T(2,128)S(1)}, u32[]{:S(2)}, u32[]{:S(2)}) async-start(s32[2,16,18]{2,0,1:T(2,128)} %copy.41), calls=%async_computation.1 | async-start | bytes 32768 | tf_op jit(solution)/shard_map/all_to_all | solution.py:155
  21.5 9.4 copy-start.8
  24.7 43.4 %all-to-all-start = ((bf16[2,128,3072]{1,0,2:T(2,128)(2,1)}), bf16[2,128,3072]{1,0,2:T(2,128)(2,1)S(1)}, u32[]{:S(2)}, u32[]{:S(2)}) async-start(bf16[2,128,3072]{1,0,2:T(2,128)(2,1)} %copy.38), calls=%async_computation | async-start | bytes 3145728 | tf_op jit(solution)/shard_map/all_to_all | solution.py:28
  31.1 12.9 %copy-start.3 = (f32[576]{0:T(1024)}, f32[576]{0:T(1024)S(1)}, u32[]{:S(2)}) copy-start(f32[576]{0:T(1024)S(1)} %select_reduce_fusion.4.weights_ref) | copy-start | bytes 6916
  68.2 125.7 %all-to-all-start.2 = ((bf16[16,18,128,128]{3,2,1,0:T(8,128)(2,1)}), bf16[16,18,128,128]{3,2,1,0:T(8,128)(2,1)}, u32[]{:S(2)}, u32[]{:S(2)}) async-start(bf16[16,18,128,128]{3,2,1,0:T(8,128)(2,1)} %gather_tiles.4), calls=%async_computation.2 | async-start | bytes 18874368 | tf_op jit(solution)/shard_map/all_to_all | solution.py:155
  223.4 147.0 %copy-start.7 = (f32[1,1536]{1,0:T(1,128)S(1)}, f32[1,1536]{1,0:T(1,128)}, u32[]{:S(2)}) copy-start(f32[1,1536]{1,0:T(1,128)} %param.18) | copy-start | bytes 18436
  223.4 357.3 %all-to-all-start.3 = ((bf16[16,18,128,128]{3,2,1,0:T(8,128)(2,1)}), bf16[16,18,128,128]{3,2,1,0:T(8,128)(2,1)}, u32[]{:S(2)}, u32[]{:S(2)}) async-start(bf16[16,18,128,128]{3,2,1,0:T(8,128)(2,1)} %gather_tiles.5), calls=%async_computation.4 | async-start | bytes 18874368 | tf_op jit(solution)/shard_map/all_to_all | solution.py:155
  228.3 352.4 %all-gather.2.cloned.1.call-start = ((), (), s32[]{:S(2)}) async-start(), calls=%async_computation.7 | async-start | bytes 7864320 | tf_op jit(solution)/shard_map/all_gather | solution.py:41
  228.4 1.0 collective-permute-start.1
  229.3 1.2 copy-start.2
  230.5 350.2 %collective-permute-start = (bf16[1536,1536]{1,0:T(8,128)(2,1)}, bf16[1536,1536]{1,0:T(8,128)(2,1)}, u32[]{:S(2)}, u32[]{:S(2)}) collective-permute-start(bf16[1536,1536]{1,0:T(8,128)(2,1)} %scatter_tiles.3), channel_id=1, source_target_pairs={{0,4},{1,5},{2,6},{3,7},{4,0},{5,1},{6,2},{7,3},{8,12},{9,13},{10,... | collective-permute-start | bytes 14155784 | tf_op jit(solution)/shard_map/ppermute | solution.py:167
  580.7 31.4 %slice-start.1 = ((s8[4718592]{0:T(1024)(128)(4,1)}), s8[524288]{0:T(1024)(128)(4,1)S(1)}, s32[]{:S(2)}) async-start(s8[4718592]{0:T(1024)(128)(4,1)} %bitcast.32), calls=%async_computation.10 | async-start | bytes 1048576
  598.0 14.1 %copy-start.1 = (bf16[1536,1536]{1,0:T(8,128)(2,1)S(1)}, bf16[1536,1536]{1,0:T(8,128)(2,1)}, u32[]{:S(2)}) copy-start(bf16[1536,1536]{1,0:T(8,128)(2,1)} %scatter_tiles.4) | copy-start | bytes 14155780
  598.0 14.1 %slice-start.2 = ((s8[4718592]{0:T(1024)(128)(4,1)}), s8[4194304]{0:T(1024)(128)(4,1)S(1)}, s32[]{:S(2)}) async-start(s8[4718592]{0:T(1024)(128)(4,1)} %bitcast.32), calls=%async_computation.11 | async-start | bytes 8388608
  635.2 229.0 %all-to-all-start.4 = ((bf16[16,18,128,128]{3,2,1,0:T(8,128)(2,1)}), bf16[16,18,128,128]{3,2,1,0:T(8,128)(2,1)}, u32[]{:S(2)}, u32[]{:S(2)}) async-start(bf16[16,18,128,128]{3,2,1,0:T(8,128)(2,1)} %gather_tiles.6), calls=%async_computation.5 | async-start | bytes 18874368 | tf_op jit(solution)/shard_map/all_to_all | solution.py:155
  647.1 204.5 %collective-permute-start.2 = (bf16[1536,1536]{1,0:T(8,128)(2,1)}, bf16[1536,1536]{1,0:T(8,128)(2,1)S(1)}, u32[]{:S(2)}, u32[]{:S(2)}) collective-permute-start(bf16[1536,1536]{1,0:T(8,128)(2,1)} %fusion.matrix_ref), channel_id=1, source_target_pairs={{0,4},{1,5},{2,6},{3,7},{4,0},{5,1},{6,2},{7,3},{8,12},{9,13},{10,... | collective-permute-start | bytes 14155784 | tf_op jit(solution)/shard_map/ppermute | solution.py:167
  851.6 2.2 copy-start
  864.2 161.6 %all-to-all-start.5 = ((bf16[16,18,128,128]{3,2,1,0:T(8,128)(2,1)}), bf16[16,18,128,128]{3,2,1,0:T(8,128)(2,1)}, u32[]{:S(2)}, u32[]{:S(2)}) async-start(bf16[16,18,128,128]{3,2,1,0:T(8,128)(2,1)} %gather_tiles.7), calls=%async_computation.6 | async-start | bytes 18874368 | tf_op jit(solution)/shard_map/all_to_all | solution.py:155
  883.6 225.1 %reduce-scatter.2.cloned.1.call-start = ((), (), s32[]{:S(2)}) async-start(), calls=%async_computation.8 | async-start | bytes 7077888 | tf_op jit(solution)/shard_map/reduce_scatter | solution.py:48
Sparse Core Ops, SparseCore 0:
  230.7 242.4 all-gather.1
  917.9 190.7 reduce-scatter.1
